TPU v7x, 32 devices: a whole 2x2x4 slice. The times are simulated.
32 devices in a mesh: tm: 8 (over y, x, core), space: 4 (over z).
Axes of the slice: x: 2, y: 2, z: 4, core: 2. Of those that a mesh axis runs over, the one named last changes fastest.
Arguments:
- latents: bfloat16 [1, 16, 16, 32, 256], P(None, 'tm', 'space'), may hold values from -24 to 24
- gain_one: float32 [256], replicated, may hold values from 0.25 to 1.75
- conv_one: bfloat16 [3, 3, 3, 256, 256], replicated, may hold values from -0.078125 to 0.078125
- gain_two: float32 [256], replicated, may hold values from 0.25 to 1.75
- conv_two: bfloat16 [3, 3, 3, 256, 256], replicated, may hold values from -0.078125 to 0.078125
- upsample: bfloat16 [3, 256, 256], replicated, may hold values from -0.375 to 0.375
Outputs:
- frames_out: bfloat16 [1, 32, 16, 32, 256], P(None, 'tm', 'space')
All inputs are finite; a program needn't handle non-finite values.
Results may differ from a plain program's by a relative error of at most 0.008.
Values may be sent and summed in bfloat16 or wider, within the bound.
A program may use at most 64 MiB of HBM per device.

v0:
```python
import jax
import jax.numpy as jnp
from jax import lax
from jax.sharding import PartitionSpec as P


def passed_along(value, axis, by):
    devices = lax.axis_size(axis)
    pairs = [(i, i + by) for i in range(devices) if 0 <= i + by < devices]
    return lax.ppermute(value, axis, pairs)


def with_halo(cells, sides, width):
    for axis, dim in sides:
        count = lax.axis_size(axis)
        ends = count - 1
        head = lax.slice_in_dim(cells, 0, width, axis=dim)
        tail = lax.slice_in_dim(cells, cells.shape[dim] - width, cells.shape[dim], axis=dim)
        cells = jnp.concatenate(
            [
                lax.ppermute(tail, axis, [(i, (i + 1) % count) for i in range(ends)]),
                cells,
                lax.ppermute(head, axis, [((i + 1) % count, i) for i in range(ends)]),
            ],
            axis=dim,
        )
    return cells


def normed_silu(features, gain_vec):
    values = features.astype(jnp.float32)
    mean_square = jnp.mean(values * values, axis=-1, keepdims=True)
    return jax.nn.silu(values * lax.rsqrt(mean_square + 1e-06) * gain_vec).astype(jnp.bfloat16)


def spatial_conv(rimmed, weight):
    widened = jnp.pad(rimmed, ((0, 0), (0, 0), (0, 0), (1, 1), (0, 0)))
    return lax.conv_general_dilated(
        widened,
        weight,
        (1, 1, 1),
        "VALID",
        dimension_numbers=("NDHWC", "DHWIO", "NDHWC"),
        preferred_element_type=jnp.float32,
    )


def with_rims(activation):
    earlier = passed_along(activation[:, -2:], "tm", 1)
    joined = jnp.concatenate([earlier, activation], axis=1)
    return with_halo(joined, (("space", 2),), 1)


def local(latents, gain_one, conv_one, gain_two, conv_two, upsample):
    first_input = normed_silu(latents, gain_one)
    hidden = spatial_conv(with_rims(first_input), conv_one).astype(jnp.bfloat16)
    second_input = normed_silu(hidden, gain_two)
    block_out = (
        latents.astype(jnp.float32) + spatial_conv(with_rims(second_input), conv_two)
    ).astype(jnp.bfloat16)
    earlier_out = passed_along(block_out[:, -1:], "tm", 1)
    previous = jnp.concatenate([earlier_out, block_out[:, :-1]], axis=1)
    channels = block_out.shape[-1]
    flat_rows = block_out.reshape(-1, channels)
    flat_previous = previous.reshape(-1, channels)
    even_frames = jnp.dot(flat_rows, upsample[0], preferred_element_type=jnp.float32)
    even_frames = even_frames + jnp.dot(
        flat_previous, upsample[1], preferred_element_type=jnp.float32
    )
    odd_frames = jnp.dot(flat_rows, upsample[2], preferred_element_type=jnp.float32)
    joined = jnp.stack(
        [even_frames.reshape(block_out.shape), odd_frames.reshape(block_out.shape)], axis=2
    )
    videos, frame_count = (block_out.shape[0], block_out.shape[1])
    return joined.reshape((videos, 2 * frame_count) + block_out.shape[2:]).astype(jnp.bfloat16)


def solution(mesh):
    return jax.shard_map(
        local,
        mesh=mesh,
        in_specs=(P(None, "tm", "space", None, None), P(), P(), P(), P(), P()),
        out_specs=P(None, "tm", "space", None, None),
        check_vma=False,
    )
```

profile of v0, /device:TPU:4, one launch (start us, length us, event | category | flops | bytes accessed | tf_op | source)
XLA Modules:
  0.0 52.6 jit_solution(13892617012004625973)
XLA Ops:
  0.0 1.2 %fusion.20 = f32[2,4,32]{1,2,0:T(8,128)S(1)} fusion(bf16[1,2,4,32,256]{4,3,2,1,0:T(8,128)(2,1)} %param.6), kind=kLoop, calls=%fused_computation.30 | loop fusion | flops 196352 | bytes 132096 | tf_op jit(solution)/shard_map/reduce_sum | solution.py:32
  1.3 1.2 %fusion.25 = bf16[1,2,4,32,256]{4,2,3,1,0:T(4,128)(2,1)S(1)} fusion(f32[256]{0:T(256)} %param.7, f32[2,4,32]{1,2,0:T(8,128)S(1)} %add_rsqrt_fusion.1, bf16[1,2,4,32,256]{4,3,2,1,0:T(8,128)(2,1)} %param.6), kind=kLoop, calls=%fused_computation.35 | loop fusion | flops 524288 | bytes 264192 | tf_op jit(solution)/shard_map/convert_element_type | solution.py:33
  2.4 1.9 %collective-permute-start = (bf16[1,2,4,32,256]{4,2,3,1,0:T(4,128)(2,1)S(1)}, bf16[1,2,4,32,256]{4,2,3,1,0:T(4,128)(2,1)S(1)}, u32[]{:S(2)}, u32[]{:S(2)}) collective-permute-start(bf16[1,2,4,32,256]{4,2,3,1,0:T(4,128)(2,1)S(1)} %fusion.25), channel_id=1, source_target_pairs={{0,4},{4,8},{8,12},{12,16},{16,20},{20,24},{24,28},{1,5},{5,9},{9,... | collective-permute-start | bytes 393224 | tf_op jit(solution)/shard_map/ppermute | solution.py:10
  4.4 5.3 %collective-permute-done = bf16[1,2,4,32,256]{4,2,3,1,0:T(4,128)(2,1)S(1)} collective-permute-done((bf16[1,2,4,32,256]{4,2,3,1,0:T(4,128)(2,1)S(1)}, bf16[1,2,4,32,256]{4,2,3,1,0:T(4,128)(2,1)S(1)}, u32[]{:S(2)}, u32[]{:S(2)}) %collective-permute-start) | collective-permute-done | bytes 131104 | tf_op jit(solution)/shard_map/ppermute | solution.py:10
  9.6 0.2 fusion.31
  9.8 3.5 %collective-permute-start.1 = (bf16[1,4,1,32,256]{4,2,3,1,0:T(2,128)(2,1)S(1)}, bf16[1,4,1,32,256]{4,2,3,1,0:T(2,128)(2,1)S(1)}, u32[]{:S(2)}, u32[]{:S(2)}) collective-permute-start(bf16[1,4,1,32,256]{4,2,3,1,0:T(2,128)(2,1)S(1)} %get-tuple-element.7), channel_id=1, source_target_pairs={{0,1},{1,2},{2,3},{4,5},{5,6},{6,7},{8,9},{9,10},{10,11},{12,13},{... | collective-permute-start | bytes 196616 | tf_op jit(solution)/shard_map/ppermute | solution.py:21
  13.3 1.3 %collective-permute-start.2 = (bf16[1,4,1,32,256]{4,2,3,1,0:T(2,128)(2,1)S(1)}, bf16[1,4,1,32,256]{4,2,3,1,0:T(2,128)(2,1)S(1)}, u32[]{:S(2)}, u32[]{:S(2)}) collective-permute-start(bf16[1,4,1,32,256]{4,2,3,1,0:T(2,128)(2,1)S(1)} %get-tuple-element.8), channel_id=1, source_target_pairs={{1,0},{2,1},{3,2},{5,4},{6,5},{7,6},{9,8},{10,9},{11,10},{13,12},{... | collective-permute-start | bytes 196616 | tf_op jit(solution)/shard_map/ppermute | solution.py:23
  14.6 1.2 %collective-permute-done.1 = bf16[1,4,1,32,256]{4,2,3,1,0:T(2,128)(2,1)S(1)} collective-permute-done((bf16[1,4,1,32,256]{4,2,3,1,0:T(2,128)(2,1)S(1)}, bf16[1,4,1,32,256]{4,2,3,1,0:T(2,128)(2,1)S(1)}, u32[]{:S(2)}, u32[]{:S(2)}) %collective-permute-start.1) | collective-permute-done | bytes 65568 | tf_op jit(solution)/shard_map/ppermute | solution.py:21
  15.8 4.4 %collective-permute-done.2 = bf16[1,4,1,32,256]{4,2,3,1,0:T(2,128)(2,1)S(1)} collective-permute-done((bf16[1,4,1,32,256]{4,2,3,1,0:T(2,128)(2,1)S(1)}, bf16[1,4,1,32,256]{4,2,3,1,0:T(2,128)(2,1)S(1)}, u32[]{:S(2)}, u32[]{:S(2)}) %collective-permute-start.2) | collective-permute-done | bytes 65568 | tf_op jit(solution)/shard_map/ppermute | solution.py:23
  20.2 0.4 maximum_bitcast_fusion
  20.6 0.3 copy.34
  21.3 1.3 %fusion.47 = (f32[2,4,8,5,256]{4,2,3,1,0:T(8,128)S(1)}, f32[2,4,8,5,256]{4,2,3,1,0:T(8,128)S(1)}) fusion(bf16[3,3,3,256,256]{4,3,2,1,0:T(8,128)(2,1)S(1)} %copy-done, bf16[4,6,1,7,2,256]{5,3,4,1,0,2:T(8,128)(2,1)S(1)} %slice.43, bf16[4,6,1,8,5,256]{5,3,4,1,0,2:T(8,128)(2,1)S(1)} %copy.22, pred[8,5]{0,1:T(8,128)(4,1)S(1)} %copy-done.5), kind=kOutput, calls=%fused_computation.70 | convolution fusion | flops 1134854144 | bytes 4857896 | tf_op jit(solution)/shard_map/conv_general_dilated | solution.py:38
  23.1 0.2 copy-done.3
  23.3 0.2 fusion.29
  23.5 1.9 %collective-permute-start.3 = (bf16[1,2,4,32,256]{4,2,3,1,0:T(4,128)(2,1)S(1)}, bf16[1,2,4,32,256]{4,2,3,1,0:T(4,128)(2,1)S(1)}, u32[]{:S(2)}, u32[]{:S(2)}) collective-permute-start(bf16[1,2,4,32,256]{4,2,3,1,0:T(4,128)(2,1)S(1)} %fusion.29), channel_id=1, source_target_pairs={{0,4},{4,8},{8,12},{12,16},{16,20},{20,24},{24,28},{1,5},{5,9},{9,... | collective-permute-start | bytes 393224 | tf_op jit(solution)/shard_map/ppermute | solution.py:10
  25.5 5.3 %collective-permute-done.3 = bf16[1,2,4,32,256]{4,2,3,1,0:T(4,128)(2,1)S(1)} collective-permute-done((bf16[1,2,4,32,256]{4,2,3,1,0:T(4,128)(2,1)S(1)}, bf16[1,2,4,32,256]{4,2,3,1,0:T(4,128)(2,1)S(1)}, u32[]{:S(2)}, u32[]{:S(2)}) %collective-permute-start.3) | collective-permute-done | bytes 131104 | tf_op jit(solution)/shard_map/ppermute | solution.py:10
  30.7 0.2 fusion.30
  30.9 3.5 %collective-permute-start.4 = (bf16[1,4,1,32,256]{4,2,3,1,0:T(2,128)(2,1)S(1)}, bf16[1,4,1,32,256]{4,2,3,1,0:T(2,128)(2,1)S(1)}, u32[]{:S(2)}, u32[]{:S(2)}) collective-permute-start(bf16[1,4,1,32,256]{4,2,3,1,0:T(2,128)(2,1)S(1)} %get-tuple-element.5), channel_id=1, source_target_pairs={{0,1},{1,2},{2,3},{4,5},{5,6},{6,7},{8,9},{9,10},{10,11},{12,13},{... | collective-permute-start | bytes 196616 | tf_op jit(solution)/shard_map/ppermute | solution.py:21
  34.4 1.3 %collective-permute-start.5 = (bf16[1,4,1,32,256]{4,2,3,1,0:T(2,128)(2,1)S(1)}, bf16[1,4,1,32,256]{4,2,3,1,0:T(2,128)(2,1)S(1)}, u32[]{:S(2)}, u32[]{:S(2)}) collective-permute-start(bf16[1,4,1,32,256]{4,2,3,1,0:T(2,128)(2,1)S(1)} %get-tuple-element.6), channel_id=1, source_target_pairs={{1,0},{2,1},{3,2},{5,4},{6,5},{7,6},{9,8},{10,9},{11,10},{13,12},{... | collective-permute-start | bytes 196616 | tf_op jit(solution)/shard_map/ppermute | solution.py:23
  35.7 1.2 %collective-permute-done.4 = bf16[1,4,1,32,256]{4,2,3,1,0:T(2,128)(2,1)S(1)} collective-permute-done((bf16[1,4,1,32,256]{4,2,3,1,0:T(2,128)(2,1)S(1)}, bf16[1,4,1,32,256]{4,2,3,1,0:T(2,128)(2,1)S(1)}, u32[]{:S(2)}, u32[]{:S(2)}) %collective-permute-start.4) | collective-permute-done | bytes 65568 | tf_op jit(solution)/shard_map/ppermute | solution.py:21
  36.9 4.4 %collective-permute-done.5 = bf16[1,4,1,32,256]{4,2,3,1,0:T(2,128)(2,1)S(1)} collective-permute-done((bf16[1,4,1,32,256]{4,2,3,1,0:T(2,128)(2,1)S(1)}, bf16[1,4,1,32,256]{4,2,3,1,0:T(2,128)(2,1)S(1)}, u32[]{:S(2)}, u32[]{:S(2)}) %collective-permute-start.5) | collective-permute-done | bytes 65568 | tf_op jit(solution)/shard_map/ppermute | solution.py:23
  41.3 0.4 maximum_bitcast_fusion.1
  41.7 0.3 copy.35
  42.0 0.2 pad.5.clone
  42.4 0.9 %copy-done.4 = bf16[3,3,3,256,256]{4,3,2,1,0:T(8,128)(2,1)S(1)} copy-done((bf16[3,3,3,256,256]{4,3,2,1,0:T(8,128)(2,1)S(1)}, bf16[3,3,3,256,256]{4,3,2,1,0:T(8,128)(2,1)}, u32[]{:S(2)}) %copy-start.4) | copy-done | bytes 3538968
  43.3 1.3 %convolution_select_fusion = f32[2,4,8,5,256]{4,2,3,1,0:T(8,128)S(1)} fusion(bf16[3,3,3,256,256]{4,3,2,1,0:T(8,128)(2,1)S(1)} %copy-done.4, bf16[4,6,1,7,2,256]{5,3,4,1,0,2:T(8,128)(2,1)S(1)} %slice.48, bf16[4,6,1,8,5,256]{5,3,4,1,0,2:T(8,128)(2,1)S(1)} %copy.27, pred[8,5]{0,1:T(8,128)(4,1)S(1)} %copy-done.5), kind=kOutput, calls=%fused_computation.4 | convolution fusion | flops 1134608384 | bytes 4530216 | tf_op jit(solution)/shard_map/conv_general_dilated | solution.py:38
  45.0 1.9 %collective-permute-start.6 = (bf16[1,1,4,32,256]{4,2,3,1,0:T(4,128)(2,1)S(1)}, bf16[1,1,4,32,256]{4,2,3,1,0:T(4,128)(2,1)S(1)}, u32[]{:S(2)}, u32[]{:S(2)}) collective-permute-start(bf16[1,1,4,32,256]{4,2,3,1,0:T(4,128)(2,1)S(1)} %get-tuple-element.9), channel_id=1, source_target_pairs={{0,4},{4,8},{8,12},{12,16},{16,20},{20,24},{24,28},{1,5},{5,9},{9,... | collective-permute-start | bytes 196616 | tf_op jit(solution)/shard_map/ppermute | solution.py:10
  47.0 0.2 fusion.34
  47.2 0.2 fusion.5
  47.4 4.2 %collective-permute-done.6 = bf16[1,1,4,32,256]{4,2,3,1,0:T(4,128)(2,1)S(1)} collective-permute-done((bf16[1,1,4,32,256]{4,2,3,1,0:T(4,128)(2,1)S(1)}, bf16[1,1,4,32,256]{4,2,3,1,0:T(4,128)(2,1)S(1)}, u32[]{:S(2)}, u32[]{:S(2)}) %collective-permute-start.6) | collective-permute-done | bytes 65568 | tf_op jit(solution)/shard_map/ppermute | solution.py:10
  51.6 0.2 fusion.4
  51.9 0.7 %copy.32 = bf16[1,2,2,4,32,256]{5,4,3,2,1,0:T(8,128)(2,1)} copy(bf16[1,2,2,4,32,256]{5,4,3,1,2,0:T(8,128)(2,1)S(1)} %pad_maximum_fusion) | data formatting | bytes 524288 | tf_op jit(solution)/shard_map/stack | solution.py:71
  (27 shorter events, 1.4 us)
Async XLA Ops:
  0.0 21.3 %copy-start = (bf16[3,3,3,256,256]{4,3,2,1,0:T(8,128)(2,1)S(1)}, bf16[3,3,3,256,256]{4,3,2,1,0:T(8,128)(2,1)}, u32[]{:S(2)}) copy-start(bf16[3,3,3,256,256]{4,3,2,1,0:T(8,128)(2,1)} %param.8) | copy-start | bytes 10616836
  2.4 7.2 %collective-permute-start = (bf16[1,2,4,32,256]{4,2,3,1,0:T(4,128)(2,1)S(1)}, bf16[1,2,4,32,256]{4,2,3,1,0:T(4,128)(2,1)S(1)}, u32[]{:S(2)}, u32[]{:S(2)}) collective-permute-start(bf16[1,2,4,32,256]{4,2,3,1,0:T(4,128)(2,1)S(1)} %fusion.25), channel_id=1, source_target_pairs={{0,4},{4,8},{8,12},{12,16},{16,20},{20,24},{24,28},{1,5},{5,9},{9,... | collective-permute-start | bytes 393224 | tf_op jit(solution)/shard_map/ppermute | solution.py:10
  9.8 6.0 %collective-permute-start.1 = (bf16[1,4,1,32,256]{4,2,3,1,0:T(2,128)(2,1)S(1)}, bf16[1,4,1,32,256]{4,2,3,1,0:T(2,128)(2,1)S(1)}, u32[]{:S(2)}, u32[]{:S(2)}) collective-permute-start(bf16[1,4,1,32,256]{4,2,3,1,0:T(2,128)(2,1)S(1)} %get-tuple-element.7), channel_id=1, source_target_pairs={{0,1},{1,2},{2,3},{4,5},{5,6},{6,7},{8,9},{9,10},{10,11},{12,13},{... | collective-permute-start | bytes 196616 | tf_op jit(solution)/shard_map/ppermute | solution.py:21
  13.3 6.9 %collective-permute-start.2 = (bf16[1,4,1,32,256]{4,2,3,1,0:T(2,128)(2,1)S(1)}, bf16[1,4,1,32,256]{4,2,3,1,0:T(2,128)(2,1)S(1)}, u32[]{:S(2)}, u32[]{:S(2)}) collective-permute-start(bf16[1,4,1,32,256]{4,2,3,1,0:T(2,128)(2,1)S(1)} %get-tuple-element.8), channel_id=1, source_target_pairs={{1,0},{2,1},{3,2},{5,4},{6,5},{7,6},{9,8},{10,9},{11,10},{13,12},{... | collective-permute-start | bytes 196616 | tf_op jit(solution)/shard_map/ppermute | solution.py:23
  20.6 0.7 %copy-start.5 = (pred[8,5]{0,1:T(8,128)(4,1)S(1)}, pred[8,5]{0,1:T(8,128)(4,1)}, u32[]{:S(2)}) copy-start(pred[8,5]{0,1:T(8,128)(4,1)} %constant.23) | copy-start | bytes 124
  22.6 0.7 %copy-start.3 = (f32[256]{0:T(256)S(1)}, f32[256]{0:T(256)}, u32[]{:S(2)}) copy-start(f32[256]{0:T(256)} %param.9) | copy-start | bytes 3076
  23.5 7.2 %collective-permute-start.3 = (bf16[1,2,4,32,256]{4,2,3,1,0:T(4,128)(2,1)S(1)}, bf16[1,2,4,32,256]{4,2,3,1,0:T(4,128)(2,1)S(1)}, u32[]{:S(2)}, u32[]{:S(2)}) collective-permute-start(bf16[1,2,4,32,256]{4,2,3,1,0:T(4,128)(2,1)S(1)} %fusion.29), channel_id=1, source_target_pairs={{0,4},{4,8},{8,12},{12,16},{16,20},{20,24},{24,28},{1,5},{5,9},{9,... | collective-permute-start | bytes 393224 | tf_op jit(solution)/shard_map/ppermute | solution.py:10
  30.9 6.0 %collective-permute-start.4 = (bf16[1,4,1,32,256]{4,2,3,1,0:T(2,128)(2,1)S(1)}, bf16[1,4,1,32,256]{4,2,3,1,0:T(2,128)(2,1)S(1)}, u32[]{:S(2)}, u32[]{:S(2)}) collective-permute-start(bf16[1,4,1,32,256]{4,2,3,1,0:T(2,128)(2,1)S(1)} %get-tuple-element.5), channel_id=1, source_target_pairs={{0,1},{1,2},{2,3},{4,5},{5,6},{6,7},{8,9},{9,10},{10,11},{12,13},{... | collective-permute-start | bytes 196616 | tf_op jit(solution)/shard_map/ppermute | solution.py:21
  34.4 6.9 %collective-permute-start.5 = (bf16[1,4,1,32,256]{4,2,3,1,0:T(2,128)(2,1)S(1)}, bf16[1,4,1,32,256]{4,2,3,1,0:T(2,128)(2,1)S(1)}, u32[]{:S(2)}, u32[]{:S(2)}) collective-permute-start(bf16[1,4,1,32,256]{4,2,3,1,0:T(2,128)(2,1)S(1)} %get-tuple-element.6), channel_id=1, source_target_pairs={{1,0},{2,1},{3,2},{5,4},{6,5},{7,6},{9,8},{10,9},{11,10},{13,12},{... | collective-permute-start | bytes 196616 | tf_op jit(solution)/shard_map/ppermute | solution.py:23
  41.3 2.0 %copy-start.4 = (bf16[3,3,3,256,256]{4,3,2,1,0:T(8,128)(2,1)S(1)}, bf16[3,3,3,256,256]{4,3,2,1,0:T(8,128)(2,1)}, u32[]{:S(2)}) copy-start(bf16[3,3,3,256,256]{4,3,2,1,0:T(8,128)(2,1)} %param.10) | copy-start | bytes 10616836
  43.3 1.5 %copy-start.1 = (bf16[1,2,4,32,256]{4,3,2,1,0:T(8,128)(2,1)S(1)}, bf16[1,2,4,32,256]{4,3,2,1,0:T(8,128)(2,1)}, u32[]{:S(2)}) copy-start(bf16[1,2,4,32,256]{4,3,2,1,0:T(8,128)(2,1)} %param.6) | copy-start | bytes 393220
  44.6 2.3 %copy-start.2 = (bf16[3,256,256]{2,1,0:T(8,128)(2,1)S(1)}, bf16[3,256,256]{2,1,0:T(8,128)(2,1)}, u32[]{:S(2)}) copy-start(bf16[3,256,256]{2,1,0:T(8,128)(2,1)} %param.11) | copy-start | bytes 1179652
  45.0 6.5 %collective-permute-start.6 = (bf16[1,1,4,32,256]{4,2,3,1,0:T(4,128)(2,1)S(1)}, bf16[1,1,4,32,256]{4,2,3,1,0:T(4,128)(2,1)S(1)}, u32[]{:S(2)}, u32[]{:S(2)}) collective-permute-start(bf16[1,1,4,32,256]{4,2,3,1,0:T(4,128)(2,1)S(1)} %get-tuple-element.9), channel_id=1, source_target_pairs={{0,4},{4,8},{8,12},{12,16},{16,20},{20,24},{24,28},{1,5},{5,9},{9,... | collective-permute-start | bytes 196616 | tf_op jit(solution)/shard_map/ppermute | solution.py:10
where the time goes:
time: 52.9 us; the launch traced here: 52.6 us
  waiting for transfers between devices  25.8 us (49%)
  starting transfers between devices  15.3 us (29%)
  other arithmetic  4.33 us (8%)
  local copies, waits for them, and re-layouts  3.62 us (7%)
  matrix products  3.21 us (6%)
    ppermute x3, waiting for transfers between devices, passed_along(): return lax.ppermute(value, axis, pairs)  14.7 us
    ppermute x2, waiting for transfers between devices, with_halo(): lax.ppermute(head, axis, [((i + 1) % count, i) for i in range(ends)])  8.73 us
    ppermute x2, starting transfers between devices, with_halo(): lax.ppermute(tail, axis, [(i, (i + 1) % count) for i in range(ends)])  6.98 us
    ppermute x3, starting transfers between devices, passed_along(): return lax.ppermute(value, axis, pairs)  5.76 us
    conv_general_dilated x2, matrix products, spatial_conv(): lax.conv_general_dilated(widened, weight, (1, 1, 1), 'VALID', dimension_n...  2.65 us
    ppermute x2, starting transfers between devices, with_halo(): lax.ppermute(head, axis, [((i + 1) % count, i) for i in range(ends)])  2.58 us
    ppermute x2, waiting for transfers between devices, with_halo(): lax.ppermute(tail, axis, [(i, (i + 1) % count) for i in range(ends)])  2.39 us
    unnamed x14, local copies, waits for them, and re-layouts  1.84 us
  transfers between devices with their start and end apart: 7, of which 7 were waited for; matrix products, arithmetic and copies ran while one was open for 1% of the time, Pallas kernels for 0%

commit v1 on v0

v1 whole, which is shorter than its diff:
```python
import functools

import jax
import jax.numpy as jnp
from jax import lax
from jax.experimental import pallas as pl
from jax.experimental.pallas import tpu as pltpu
from jax.sharding import PartitionSpec as P

MESH = pl.DeviceIdType.MESH
WAYS = ((1, 0), (1, 1), (1, -1), (0, 1), (0, -1))


def normed_silu(values, gain):
    mean_square = jnp.mean(values * values, axis=-1, keepdims=True)
    scaled = values * lax.rsqrt(mean_square + 1e-06) * gain
    return (scaled * jax.nn.sigmoid(scaled)).astype(jnp.bfloat16)


def shifted(total, by, rows, width):
    cells, channels = total.shape
    column = lax.broadcasted_iota(jnp.int32, total.shape, 0) % width
    if by > 0:
        return jnp.where(column == 0, 0.0, pltpu.roll(total, 1, 0))
    return jnp.where(column == width - 1, 0.0, pltpu.roll(total, cells - 1, 0))


def kernel(
    tiles, lat, g1, w1, g2, w2, up, out,
    lbuf, g1buf, g2buf, w1buf, w2buf, ubuf, x1, x2, blocks, previous, obuf,
    load_sem, w1_sem, w2_sem, out_sem, send_sem, recv_sem, last_sem,
):
    T, S = tiles
    _, F, R, W, C = lat.shape
    t, s = lax.axis_index("tm"), lax.axis_index("space")

    loads = [
        pltpu.make_async_copy(lat.at[0], lbuf, load_sem.at[0]),
        pltpu.make_async_copy(g1, g1buf, load_sem.at[1]),
        pltpu.make_async_copy(g2, g2buf, load_sem.at[2]),
        pltpu.make_async_copy(up, ubuf, load_sem.at[3]),
    ]
    w_loads = [
        {dt: pltpu.make_async_copy(w.at[dt], buf.at[dt], sem.at[dt]) for dt in (2, 1, 0)}
        for w, buf, sem in ((w1, w1buf, w1_sem), (w2, w2buf, w2_sem))
    ]
    loads[0].start()
    loads[1].start()
    for dt in (2, 1, 0):
        w_loads[0][dt].start()
    loads[2].start()
    for dt in (2, 1, 0):
        w_loads[1][dt].start()
    loads[3].start()

    def inside(dt, ds):
        checks = []
        if dt > 0:
            checks.append(t < T - 1)
        if dt < 0:
            checks.append(t > 0)
        if ds > 0:
            checks.append(s < S - 1)
        if ds < 0:
            checks.append(s > 0)
        return functools.reduce(jnp.logical_and, checks)

    def there(dt, ds):
        return (t + dt, s + ds)

    barrier = pltpu.get_barrier_semaphore()
    for dt, ds in WAYS:
        @pl.when(inside(-dt, -ds))
        def _():
            pl.semaphore_signal(barrier, inc=1, device_id=there(-dt, -ds), device_id_type=MESH)

    def message(k, x, a, way):
        dt, ds = WAYS[way]
        src_rows = {0: pl.ds(1, R), 1: pl.ds(R, 1), -1: pl.ds(1, 1)}[ds]
        dst_rows = {0: pl.ds(1, R), 1: pl.ds(0, 1), -1: pl.ds(R + 1, 1)}[ds]
        dst_frame = a - (F - 2) if dt else 2 + a
        return pltpu.make_async_remote_copy(
            src_ref=x.at[2 + a, src_rows],
            dst_ref=x.at[dst_frame, dst_rows],
            send_sem=send_sem.at[k, a, way],
            recv_sem=recv_sem.at[k, a, way],
            device_id=there(dt, ds),
            device_id_type=MESH,
        )

    def ways_of(a):
        return [way for way, (dt, _) in enumerate(WAYS) if dt == 0 or a >= F - 2]

    def send(k, x, a):
        for way in ways_of(a):
            @pl.when(inside(*WAYS[way]))
            def _():
                message(k, x, a, way).start()

    def sent(k, x, a):
        for way in ways_of(a):
            @pl.when(inside(*WAYS[way]))
            def _():
                message(k, x, a, way).wait_send()

    arrived = set()

    def receive(k, x, frame):
        if (k, frame) in arrived:
            return
        arrived.add((k, frame))
        early = frame < 2
        a = frame + F - 2 if early else frame - 2
        for way in ways_of(a):
            dt, ds = WAYS[way]
            if (dt > 0) == early:
                @pl.when(inside(-dt, -ds))
                def _():
                    message(k, x, a, way).wait_recv()

    zero_row = jnp.zeros((F + 2, 1, W, C), jnp.bfloat16)
    for x in (x1, x2):
        @pl.when(t == 0)
        def _():
            x[0:2] = jnp.zeros((2, R + 2, W, C), jnp.bfloat16)

        @pl.when(s == 0)
        def _():
            x[:, 0:1] = zero_row

        @pl.when(s == S - 1)
        def _():
            x[:, R + 1 : R + 2] = zero_row

    @pl.when(t == 0)
    def _():
        previous[...] = jnp.zeros((R * W, C), jnp.bfloat16)

    order = list(reversed(range(F)))
    loads[0].wait()
    loads[1].wait()
    for n, a in enumerate(order):
        values = lbuf[a].reshape(R * W, C).astype(jnp.float32)
        x1[2 + a, 1 : R + 1] = normed_silu(values, g1buf[...]).reshape(R, W, C)
        if n == 0:
            targets = sum(inside(*way).astype(jnp.int32) for way in WAYS)
            pl.semaphore_wait(barrier, targets)
        send(0, x1, a)

    loaded = set()

    def conv(k, x, wbuf, a):
        totals = [None] * 3
        for dt in (2, 1, 0):
            if (k, dt) not in loaded:
                loaded.add((k, dt))
                w_loads[k][dt].wait()
            receive(k, x, a + dt)
            cells = jnp.concatenate(
                [x[a + dt, di : di + R].reshape(R * W, C) for di in range(3)], axis=1
            )
            for dj in range(3):
                taps = jnp.concatenate([wbuf[dt, di, dj] for di in range(3)], axis=0)
                part = jnp.dot(cells, taps, preferred_element_type=jnp.float32)
                totals[dj] = part if totals[dj] is None else totals[dj] + part
        return shifted(totals[0], 1, R, W) + totals[1] + shifted(totals[2], -1, R, W)

    for n, a in enumerate(order):
        hidden = conv(0, x1, w1buf, a).astype(jnp.bfloat16).astype(jnp.float32)
        if n == 0:
            loads[2].wait()
        x2[2 + a, 1 : R + 1] = normed_silu(hidden, g2buf[...]).reshape(R, W, C)
        send(1, x2, a)

    last = pltpu.make_async_remote_copy(
        src_ref=blocks.at[F - 1], dst_ref=previous,
        send_sem=last_sem.at[0], recv_sem=last_sem.at[1],
        device_id=there(1, 0), device_id_type=MESH,
    )
    for n, a in enumerate(order):
        total = conv(1, x2, w2buf, a) + lbuf[a].reshape(R * W, C).astype(jnp.float32)
        blocks[a] = total.astype(jnp.bfloat16)
        if n == 0:
            @pl.when(inside(1, 0))
            def _():
                last.start()

    loads[3].wait()
    stores = [pltpu.make_async_copy(obuf.at[j], out.at[0, j], out_sem.at[j]) for j in range(2 * F)]

    def put(j, value):
        obuf[j] = value.astype(jnp.bfloat16).reshape(R, W, C)
        stores[j].start()

    def product(rows, m):
        return jnp.dot(rows, ubuf[m], preferred_element_type=jnp.float32)

    for a in order:
        put(2 * a + 1, product(blocks[a], 2))
        if a:
            put(2 * a, product(blocks[a], 0) + product(blocks[a - 1], 1))
    first = product(blocks[0], 0)

    @pl.when(inside(-1, 0))
    def _():
        last.wait_recv()

    put(0, first + product(previous[...], 1))

    for k, x in enumerate((x1, x2)):
        for a in order:
            sent(k, x, a)

    @pl.when(inside(1, 0))
    def _():
        last.wait_send()

    for store in stores:
        store.wait()


def local(tiles, latents, gain_one, conv_one, gain_two, conv_two, upsample):
    videos, F, R, W, C = latents.shape
    assert videos == 1 and F >= 2
    anywhere = pl.BlockSpec(memory_space=pl.ANY)
    in_hbm = pl.BlockSpec(memory_space=pltpu.HBM)
    bf16, f32 = jnp.bfloat16, jnp.float32
    return pl.pallas_call(
        functools.partial(kernel, tiles),
        out_shape=jax.ShapeDtypeStruct((1, 2 * F, R, W, C), bf16),
        in_specs=[in_hbm] * 6,
        out_specs=anywhere,
        scratch_shapes=[
            pltpu.VMEM((F, R, W, C), bf16),
            pltpu.VMEM((1, C), f32),
            pltpu.VMEM((1, C), f32),
            pltpu.VMEM(conv_one.shape, bf16),
            pltpu.VMEM(conv_two.shape, bf16),
            pltpu.VMEM(upsample.shape, bf16),
            pltpu.VMEM((F + 2, R + 2, W, C), bf16),
            pltpu.VMEM((F + 2, R + 2, W, C), bf16),
            pltpu.VMEM((F, R * W, C), bf16),
            pltpu.VMEM((R * W, C), bf16),
            pltpu.VMEM((2 * F, R, W, C), bf16),
            pltpu.SemaphoreType.DMA((4,)),
            pltpu.SemaphoreType.DMA((3,)),
            pltpu.SemaphoreType.DMA((3,)),
            pltpu.SemaphoreType.DMA((2 * F,)),
            pltpu.SemaphoreType.DMA((2, F, len(WAYS))),
            pltpu.SemaphoreType.DMA((2, F, len(WAYS))),
            pltpu.SemaphoreType.DMA((2,)),
        ],
        compiler_params=pltpu.CompilerParams(
            collective_id=0, has_side_effects=True, vmem_limit_bytes=56 * 2**20
        ),
        cost_estimate=pl.CostEstimate(
            flops=2 * F * R * W * C * C * 57, bytes_accessed=8 * 2**20, transcendentals=4 * F * R * W * C
        ),
    )(latents, gain_one.reshape(1, C), conv_one, gain_two.reshape(1, C), conv_two, upsample)


def solution(mesh):
    tiles = (mesh.shape["tm"], mesh.shape["space"])
    return jax.shard_map(
        functools.partial(local, tiles),
        mesh=mesh,
        in_specs=(P(None, "tm", "space", None, None), P(), P(), P(), P(), P()),
        out_specs=P(None, "tm", "space", None, None),
        check_vma=False,
    )
```

time: 52.9 us -> 17.7 us (0.33)
  waiting for transfers between devices: 25.8 us -> 0 us
  Pallas kernels: 0 us -> 15.8 us
  starting transfers between devices: 15.3 us -> 0 us
  other arithmetic: 4.33 us -> 0 us
  matrix products: 3.21 us -> 0 us
  local copies, waits for them, and re-layouts: 3.62 us -> 1.67 us
    ppermute x7 -> x0, waiting for transfers between devices: 25.8 us -> none  [the longest x3 14.7 us: passed_along(): return lax.ppermute(value, axis, pairs)]
    pallas_call x0 -> x1, Pallas kernels: none -> 15.8 us  [local(): pl.pallas_call(functools.partial(kernel, tiles), out_shape=jax.ShapeDtype...]
    ppermute x7 -> x0, starting transfers between devices: 15.3 us -> none  [the longest x2 6.98 us: with_halo(): lax.ppermute(tail, axis, [(i, (i + 1) % count) for i in range(ends)])]
    conv_general_dilated x2 -> x0, matrix products: 2.65 us -> none  [spatial_conv(): lax.conv_general_dilated(widened, weight, (1, 1, 1), 'VALID', dimension_n...]
    convert_element_type x3 -> x0, other arithmetic: 1.53 us -> none  [the longest x2 1.39 us: normed_silu(): jax.nn.silu(values * lax.rsqrt(mean_square + 1e-06) * gain_vec)]
    concatenate x5 -> x0, other arithmetic: 1.37 us -> none  [the longest x2 0.86 us: with_halo(): jnp.concatenate([lax.ppermute(tail, axis, [(i, (i + 1) % count) for i in...]
    reduce_sum x2 -> x0, other arithmetic: 1.37 us -> none  [normed_silu(): mean_square = jnp.mean(values * values, axis=-1, keepdims=True)]
    another operation x1 -> x0, local copies, waits for them, and re-layouts: 0.72 us -> none  [local(): jnp.stack([even_frames.reshape(block_out.shape), odd_frames.reshape(block...]
  transfers between devices with their start and end apart: 7 -> 0, of which waited for: 7 -> 0; matrix products, arithmetic and copies ran while one was open for 1% -> 0% of each run, Pallas kernels for 0% -> 0%
where the time goes in v1:
time: 17.7 us; the launch traced here: 17.4 us
  Pallas kernels  15.8 us (89%)
  local copies, waits for them, and re-layouts  1.67 us (9%)
    pallas_call x1, Pallas kernels, local(): pl.pallas_call(functools.partial(kernel, tiles), out_shape=jax.ShapeDtype...  15.8 us
    unnamed x1, local copies, waits for them, and re-layouts  1.67 us

profile of v1, /device:TPU:4, one launch (start us, length us, event | category | flops | bytes accessed | tf_op | source)
XLA Modules:
  0.0 17.4 jit_solution(1355887018616797907)
XLA Ops:
  0.0 15.8 %shard_map.64 = bf16[1,4,4,32,256]{4,3,2,1,0:T(8,128)(2,1)} custom-call(bf16[1,2,4,32,256]{4,3,2,1,0:T(8,128)(2,1)} %lat.1, f32[1,256]{1,0:T(1,128)} %bitcast.2, bf16[3,3,3,256,256]{4,3,2,1,0:T(8,128)(2,1)} %w1.1, f32[1,256]{1,0:T(1,128)} %bitcast.3, bf16[3,3,3,256,256]{4,3,2,1,0:T(8,128)(2,1)} %w2.1, bf16[3,256,256]{2,1,0:T(8,128)(2,1)} %up.1), custom_call_target="tpu_custom_call" | custom-call | flops 1912602624 | bytes 8388608 | tf_op jit(solution)/shard_map/pallas_call | solution.py:228
  15.8 1.7 %copy.8 = bf16[1,4,4,32,256]{4,3,2,1,0:T(8,128)(2,1)} copy(bf16[1,4,4,32,256]{4,3,2,1,0:T(8,128)(2,1)} %shard_map.64) | data formatting | bytes 524288

commit v2 on v1

--- a/solution.py
+++ b/solution.py
@@ -27,8 +27,8 @@
 
 def kernel(
     tiles, lat, g1, w1, g2, w2, up, out,
-    lbuf, g1buf, g2buf, w1buf, w2buf, ubuf, x1, x2, blocks, previous, obuf,
-    load_sem, w1_sem, w2_sem, out_sem, send_sem, recv_sem, last_sem,
+    lbuf, g1buf, g2buf, w1buf, w2buf, ubuf, x1, x2, blocks, previous,
+    load_sem, w1_sem, w2_sem, send_sem, recv_sem, last_sem,
 ):
     T, S = tiles
     _, F, R, W, C = lat.shape
@@ -186,11 +186,9 @@
                 last.start()
 
     loads[3].wait()
-    stores = [pltpu.make_async_copy(obuf.at[j], out.at[0, j], out_sem.at[j]) for j in range(2 * F)]
 
     def put(j, value):
-        obuf[j] = value.astype(jnp.bfloat16).reshape(R, W, C)
-        stores[j].start()
+        out[0, j] = value.astype(jnp.bfloat16).reshape(R, W, C)
 
     def product(rows, m):
         return jnp.dot(rows, ubuf[m], preferred_element_type=jnp.float32)
@@ -215,21 +213,17 @@
     def _():
         last.wait_send()
 
-    for store in stores:
-        store.wait()
-
 
 def local(tiles, latents, gain_one, conv_one, gain_two, conv_two, upsample):
     videos, F, R, W, C = latents.shape
     assert videos == 1 and F >= 2
-    anywhere = pl.BlockSpec(memory_space=pl.ANY)
     in_hbm = pl.BlockSpec(memory_space=pltpu.HBM)
     bf16, f32 = jnp.bfloat16, jnp.float32
     return pl.pallas_call(
         functools.partial(kernel, tiles),
-        out_shape=jax.ShapeDtypeStruct((1, 2 * F, R, W, C), bf16),
+        out_shape=pltpu.VMEM((1, 2 * F, R, W, C), bf16),
         in_specs=[in_hbm] * 6,
-        out_specs=anywhere,
+        out_specs=pl.BlockSpec(memory_space=pltpu.VMEM),
         scratch_shapes=[
             pltpu.VMEM((F, R, W, C), bf16),
             pltpu.VMEM((1, C), f32),
@@ -241,11 +235,9 @@
             pltpu.VMEM((F + 2, R + 2, W, C), bf16),
             pltpu.VMEM((F, R * W, C), bf16),
             pltpu.VMEM((R * W, C), bf16),
-            pltpu.VMEM((2 * F, R, W, C), bf16),
             pltpu.SemaphoreType.DMA((4,)),
             pltpu.SemaphoreType.DMA((3,)),
             pltpu.SemaphoreType.DMA((3,)),
-            pltpu.SemaphoreType.DMA((2 * F,)),
             pltpu.SemaphoreType.DMA((2, F, len(WAYS))),
             pltpu.SemaphoreType.DMA((2, F, len(WAYS))),
             pltpu.SemaphoreType.DMA((2,)),

time: 17.7 us -> 16.1 us (0.910)
  local copies, waits for them, and re-layouts: 1.67 us -> 0.71 us
  Pallas kernels: 15.8 us -> 15.1 us
    unnamed x1, local copies, waits for them, and re-layouts: 1.67 us -> 0.71 us
    pallas_call x1, Pallas kernels: 15.8 us -> 15.1 us  [local(): pl.pallas_call(functools.partial(kernel, tiles), out_shape=pltpu.VMEM((1,...]
where the time goes in v2:
time: 16.1 us; the launch traced here: 15.8 us
  Pallas kernels  15.1 us (94%)
  local copies, waits for them, and re-layouts  0.71 us (4%)
    pallas_call x1, Pallas kernels, local(): pl.pallas_call(functools.partial(kernel, tiles), out_shape=pltpu.VMEM((1,...  15.1 us
    unnamed x1, local copies, waits for them, and re-layouts  0.71 us

profile of v2, /device:TPU:4, one launch (start us, length us, event | category | flops | bytes accessed | tf_op | source)
XLA Modules:
  0.0 15.8 jit_solution(8492571831660603298)
XLA Ops:
  0.0 15.1 %shard_map.64 = bf16[1,4,4,32,256]{4,3,2,1,0:T(8,128)(2,1)S(1)} custom-call(bf16[1,2,4,32,256]{4,3,2,1,0:T(8,128)(2,1)} %lat.1, f32[1,256]{1,0:T(1,128)} %bitcast.2, bf16[3,3,3,256,256]{4,3,2,1,0:T(8,128)(2,1)} %w1.1, f32[1,256]{1,0:T(1,128)} %bitcast.3, bf16[3,3,3,256,256]{4,3,2,1,0:T(8,128)(2,1)} %w2.1, bf16[3,256,256]{2,1,0:T(8,128)(2,1)} %up.1), custom_call_target="tpu_custom_call" | custom-call | flops 1912602624 | bytes 8388608 | tf_op jit(solution)/shard_map/pallas_call | solution.py:222
  15.1 0.7 %copy.8 = bf16[1,4,4,32,256]{4,3,2,1,0:T(8,128)(2,1)} copy(bf16[1,4,4,32,256]{4,3,2,1,0:T(8,128)(2,1)S(1)} %shard_map.64) | data formatting | bytes 524288

commit v3 on v2

--- a/solution.py
+++ b/solution.py
@@ -8,7 +8,7 @@
 from jax.sharding import PartitionSpec as P
 
 MESH = pl.DeviceIdType.MESH
-WAYS = ((1, 0), (1, 1), (1, -1), (0, 1), (0, -1))
+WAYS = ((0, 1), (0, -1), (1, 0), (1, 1), (1, -1))
 
 
 def normed_silu(values, gain):
@@ -149,25 +149,43 @@
 
     loaded = set()
 
-    def conv(k, x, wbuf, a):
-        totals = [None] * 3
-        for dt in (2, 1, 0):
+    def conv(k, x, wbuf):
+        totals = {}
+
+        def add(frames, dt):
             if (k, dt) not in loaded:
                 loaded.add((k, dt))
                 w_loads[k][dt].wait()
-            receive(k, x, a + dt)
+            low, count = frames[0], len(frames)
+            for a in frames:
+                receive(k, x, a + dt)
             cells = jnp.concatenate(
-                [x[a + dt, di : di + R].reshape(R * W, C) for di in range(3)], axis=1
+                [
+                    x[low + dt : low + dt + count, di : di + R].reshape(count * R * W, C)
+                    for di in range(3)
+                ],
+                axis=1,
             )
             for dj in range(3):
                 taps = jnp.concatenate([wbuf[dt, di, dj] for di in range(3)], axis=0)
                 part = jnp.dot(cells, taps, preferred_element_type=jnp.float32)
-                totals[dj] = part if totals[dj] is None else totals[dj] + part
-        return shifted(totals[0], 1, R, W) + totals[1] + shifted(totals[2], -1, R, W)
-
-    for n, a in enumerate(order):
-        hidden = conv(0, x1, w1buf, a).astype(jnp.bfloat16).astype(jnp.float32)
-        if n == 0:
+                for n, a in enumerate(frames):
+                    piece = part[n * R * W : (n + 1) * R * W]
+                    totals[a, dj] = totals[a, dj] + piece if (a, dj) in totals else piece
+
+        for dt in (2, 1, 0):
+            frames = [a for a in range(F) if a + dt >= 2]
+            if frames:
+                add(frames, dt)
+        for a in order:
+            for dt in (1, 0):
+                if a + dt < 2:
+                    add([a], dt)
+            yield a, shifted(totals[a, 0], 1, R, W) + totals[a, 1] + shifted(totals[a, 2], -1, R, W)
+
+    for a, total in conv(0, x1, w1buf):
+        hidden = total.astype(jnp.bfloat16).astype(jnp.float32)
+        if a == F - 1:
             loads[2].wait()
         x2[2 + a, 1 : R + 1] = normed_silu(hidden, g2buf[...]).reshape(R, W, C)
         send(1, x2, a)
@@ -177,10 +195,10 @@
         send_sem=last_sem.at[0], recv_sem=last_sem.at[1],
         device_id=there(1, 0), device_id_type=MESH,
     )
-    for n, a in enumerate(order):
-        total = conv(1, x2, w2buf, a) + lbuf[a].reshape(R * W, C).astype(jnp.float32)
+    for a, total in conv(1, x2, w2buf):
+        total = total + lbuf[a].reshape(R * W, C).astype(jnp.float32)
         blocks[a] = total.astype(jnp.bfloat16)
-        if n == 0:
+        if a == F - 1:
             @pl.when(inside(1, 0))
             def _():
                 last.start()

time: 16.1 us -> 16.8 us (1.043)
  Pallas kernels: 15.1 us -> 15.9 us
    pallas_call x1, Pallas kernels: 15.1 us -> 15.9 us  [local(): pl.pallas_call(functools.partial(kernel, tiles), out_shape=pltpu.VMEM((1,...]
where the time goes in v3:
time: 16.8 us; the launch traced here: 16.7 us
  Pallas kernels  15.9 us (95%)
  local copies, waits for them, and re-layouts  0.71 us (4%)
    pallas_call x1, Pallas kernels, local(): pl.pallas_call(functools.partial(kernel, tiles), out_shape=pltpu.VMEM((1,...  15.9 us
    unnamed x1, local copies, waits for them, and re-layouts  0.71 us

profile of v3, /device:TPU:4, one launch (start us, length us, event | category | flops | bytes accessed | tf_op | source)
XLA Modules:
  0.0 16.7 jit_solution(7292598063757001542)
XLA Ops:
  0.0 15.9 %shard_map.64 = bf16[1,4,4,32,256]{4,3,2,1,0:T(8,128)(2,1)S(1)} custom-call(bf16[1,2,4,32,256]{4,3,2,1,0:T(8,128)(2,1)} %lat.1, f32[1,256]{1,0:T(1,128)} %bitcast.2, bf16[3,3,3,256,256]{4,3,2,1,0:T(8,128)(2,1)} %w1.1, f32[1,256]{1,0:T(1,128)} %bitcast.3, bf16[3,3,3,256,256]{4,3,2,1,0:T(8,128)(2,1)} %w2.1, bf16[3,256,256]{2,1,0:T(8,128)(2,1)} %up.1), custom_call_target="tpu_custom_call" | custom-call | flops 1912602624 | bytes 8388608 | tf_op jit(solution)/shard_map/pallas_call | solution.py:240
  15.9 0.7 %copy.8 = bf16[1,4,4,32,256]{4,3,2,1,0:T(8,128)(2,1)} copy(bf16[1,4,4,32,256]{4,3,2,1,0:T(8,128)(2,1)S(1)} %shard_map.64) | data formatting | bytes 524288

commit v4 on v2

--- a/solution.py
+++ b/solution.py
@@ -49,9 +49,6 @@
     for dt in (2, 1, 0):
         w_loads[0][dt].start()
     loads[2].start()
-    for dt in (2, 1, 0):
-        w_loads[1][dt].start()
-    loads[3].start()
 
     def inside(dt, ds):
         checks = []
@@ -146,6 +143,10 @@
             targets = sum(inside(*way).astype(jnp.int32) for way in WAYS)
             pl.semaphore_wait(barrier, targets)
         send(0, x1, a)
+
+    for dt in (2, 1, 0):
+        w_loads[1][dt].start()
+    loads[3].start()
 
     loaded = set()
 

time: 16.1 us -> 16.1 us (level)
  no operation moved by 1% of the time
where the time goes in v4:
time: 16.1 us; the launch traced here: 15.8 us
  Pallas kernels  15.1 us (94%)
  local copies, waits for them, and re-layouts  0.71 us (4%)
    pallas_call x1, Pallas kernels, local(): pl.pallas_call(functools.partial(kernel, tiles), out_shape=pltpu.VMEM((1,...  15.1 us
    unnamed x1, local copies, waits for them, and re-layouts  0.71 us

profile of v4, /device:TPU:4, one launch (start us, length us, event | category | flops | bytes accessed | tf_op | source)
XLA Modules:
  0.0 15.8 jit_solution(12468736810460554321)
XLA Ops:
  0.0 15.1 %shard_map.64 = bf16[1,4,4,32,256]{4,3,2,1,0:T(8,128)(2,1)S(1)} custom-call(bf16[1,2,4,32,256]{4,3,2,1,0:T(8,128)(2,1)} %lat.1, f32[1,256]{1,0:T(1,128)} %bitcast.2, bf16[3,3,3,256,256]{4,3,2,1,0:T(8,128)(2,1)} %w1.1, f32[1,256]{1,0:T(1,128)} %bitcast.3, bf16[3,3,3,256,256]{4,3,2,1,0:T(8,128)(2,1)} %w2.1, bf16[3,256,256]{2,1,0:T(8,128)(2,1)} %up.1), custom_call_target="tpu_custom_call" | custom-call | flops 1912602624 | bytes 8388608 | tf_op jit(solution)/shard_map/pallas_call | solution.py:223
  15.1 0.7 %copy.8 = bf16[1,4,4,32,256]{4,3,2,1,0:T(8,128)(2,1)} copy(bf16[1,4,4,32,256]{4,3,2,1,0:T(8,128)(2,1)S(1)} %shard_map.64) | data formatting | bytes 524288

commit v5 on v2

--- a/solution.py
+++ b/solution.py
@@ -8,7 +8,7 @@
 from jax.sharding import PartitionSpec as P
 
 MESH = pl.DeviceIdType.MESH
-WAYS = ((1, 0), (1, 1), (1, -1), (0, 1), (0, -1))
+WAYS = ((0, 1), (0, -1), (1, 0), (1, 1), (1, -1))
 
 
 def normed_silu(values, gain):

time: 16.1 us -> 16.1 us (level)
  no operation moved by 1% of the time
where the time goes in v5:
time: 16.1 us; the launch traced here: 15.9 us
  Pallas kernels  15.2 us (94%)
  local copies, waits for them, and re-layouts  0.71 us (4%)
    pallas_call x1, Pallas kernels, local(): pl.pallas_call(functools.partial(kernel, tiles), out_shape=pltpu.VMEM((1,...  15.2 us
    unnamed x1, local copies, waits for them, and re-layouts  0.71 us

profile of v5, /device:TPU:4, one launch (start us, length us, event | category | flops | bytes accessed | tf_op | source)
XLA Modules:
  0.0 15.9 jit_solution(7993133515968403877)
XLA Ops:
  0.0 15.2 %shard_map.64 = bf16[1,4,4,32,256]{4,3,2,1,0:T(8,128)(2,1)S(1)} custom-call(bf16[1,2,4,32,256]{4,3,2,1,0:T(8,128)(2,1)} %lat.1, f32[1,256]{1,0:T(1,128)} %bitcast.2, bf16[3,3,3,256,256]{4,3,2,1,0:T(8,128)(2,1)} %w1.1, f32[1,256]{1,0:T(1,128)} %bitcast.3, bf16[3,3,3,256,256]{4,3,2,1,0:T(8,128)(2,1)} %w2.1, bf16[3,256,256]{2,1,0:T(8,128)(2,1)} %up.1), custom_call_target="tpu_custom_call" | custom-call | flops 1912602624 | bytes 8388608 | tf_op jit(solution)/shard_map/pallas_call | solution.py:222
  15.2 0.7 %copy.8 = bf16[1,4,4,32,256]{4,3,2,1,0:T(8,128)(2,1)} copy(bf16[1,4,4,32,256]{4,3,2,1,0:T(8,128)(2,1)S(1)} %shard_map.64) | data formatting | bytes 524288

commit v6 on v2

--- a/solution.py
+++ b/solution.py
@@ -41,16 +41,24 @@
         pltpu.make_async_copy(up, ubuf, load_sem.at[3]),
     ]
     w_loads = [
-        {dt: pltpu.make_async_copy(w.at[dt], buf.at[dt], sem.at[dt]) for dt in (2, 1, 0)}
+        {
+            dt: [
+                pltpu.make_async_copy(w.at[dt, :, dj], buf.at[dt, dj], sem.at[dt, dj])
+                for dj in range(3)
+            ]
+            for dt in (2, 1, 0)
+        }
         for w, buf, sem in ((w1, w1buf, w1_sem), (w2, w2buf, w2_sem))
     ]
     loads[0].start()
     loads[1].start()
     for dt in (2, 1, 0):
-        w_loads[0][dt].start()
+        for load in w_loads[0][dt]:
+            load.start()
     loads[2].start()
     for dt in (2, 1, 0):
-        w_loads[1][dt].start()
+        for load in w_loads[1][dt]:
+            load.start()
     loads[3].start()
 
     def inside(dt, ds):
@@ -154,13 +162,14 @@
         for dt in (2, 1, 0):
             if (k, dt) not in loaded:
                 loaded.add((k, dt))
-                w_loads[k][dt].wait()
+                for load in w_loads[k][dt]:
+                    load.wait()
             receive(k, x, a + dt)
             cells = jnp.concatenate(
                 [x[a + dt, di : di + R].reshape(R * W, C) for di in range(3)], axis=1
             )
             for dj in range(3):
-                taps = jnp.concatenate([wbuf[dt, di, dj] for di in range(3)], axis=0)
+                taps = wbuf[dt, dj].reshape(3 * C, C)
                 part = jnp.dot(cells, taps, preferred_element_type=jnp.float32)
                 totals[dj] = part if totals[dj] is None else totals[dj] + part
         return shifted(totals[0], 1, R, W) + totals[1] + shifted(totals[2], -1, R, W)
@@ -236,8 +245,8 @@
             pltpu.VMEM((F, R * W, C), bf16),
             pltpu.VMEM((R * W, C), bf16),
             pltpu.SemaphoreType.DMA((4,)),
-            pltpu.SemaphoreType.DMA((3,)),
-            pltpu.SemaphoreType.DMA((3,)),
+            pltpu.SemaphoreType.DMA((3, 3)),
+            pltpu.SemaphoreType.DMA((3, 3)),
             pltpu.SemaphoreType.DMA((2, F, len(WAYS))),
             pltpu.SemaphoreType.DMA((2, F, len(WAYS))),
             pltpu.SemaphoreType.DMA((2,)),

time: 16.1 us -> 16.8 us (1.043)
  Pallas kernels: 15.1 us -> 15.9 us
    pallas_call x1, Pallas kernels: 15.1 us -> 15.9 us  [local(): pl.pallas_call(functools.partial(kernel, tiles), out_shape=pltpu.VMEM((1,...]
where the time goes in v6:
time: 16.8 us; the launch traced here: 16.6 us
  Pallas kernels  15.9 us (95%)
  local copies, waits for them, and re-layouts  0.71 us (4%)
    pallas_call x1, Pallas kernels, local(): pl.pallas_call(functools.partial(kernel, tiles), out_shape=pltpu.VMEM((1,...  15.9 us
    unnamed x1, local copies, waits for them, and re-layouts  0.71 us

profile of v6, /device:TPU:4, one launch (start us, length us, event | category | flops | bytes accessed | tf_op | source)
XLA Modules:
  0.0 16.6 jit_solution(10346024872165032294)
XLA Ops:
  0.0 15.9 %shard_map.64 = bf16[1,4,4,32,256]{4,3,2,1,0:T(8,128)(2,1)S(1)} custom-call(bf16[1,2,4,32,256]{4,3,2,1,0:T(8,128)(2,1)} %lat.1, f32[1,256]{1,0:T(1,128)} %bitcast.2, bf16[3,3,3,256,256]{4,3,2,1,0:T(8,128)(2,1)} %w1.1, f32[1,256]{1,0:T(1,128)} %bitcast.3, bf16[3,3,3,256,256]{4,3,2,1,0:T(8,128)(2,1)} %w2.1, bf16[3,256,256]{2,1,0:T(8,128)(2,1)} %up.1), custom_call_target="tpu_custom_call" | custom-call | flops 1912602624 | bytes 8388608 | tf_op jit(solution)/shard_map/pallas_call | solution.py:231
  15.9 0.7 %copy.8 = bf16[1,4,4,32,256]{4,3,2,1,0:T(8,128)(2,1)} copy(bf16[1,4,4,32,256]{4,3,2,1,0:T(8,128)(2,1)S(1)} %shard_map.64) | data formatting | bytes 524288
